TPU v7x, 256 devices: a whole 4x4x8 slice. The times are simulated.
256 devices in a mesh: ctx: 32 (over z, x), head: 8 (over y, core).
Axes of the slice: x: 4, y: 4, z: 8, core: 2. Of those that a mesh axis runs over, the one named last changes fastest.
Arguments:
- tokens: bfloat16 [32768, 2048], P(('ctx', 'head')), may hold values from -6 to 6
- projection: bfloat16 [2048, 4096], P(None, 'head'), may hold values from -0.125 to 0.125
- context_state: float32 [16, 2080, 64], P('head'), may hold values from -24 to 24
- norm_gain: float32 [2048], P('head'), may hold values from 0.1 to 1.9
Outputs:
- retained: bfloat16 [32768, 2048], P(('ctx', 'head'))
All inputs are finite; a program needn't handle non-finite values.
Results may differ from a plain program's by a relative error of at most 0.008.
Values may be sent and summed in bfloat16 or wider, within the bound.
A program may use at most 192 MiB of HBM per device.

v0:
```python
import math

import jax
import jax.numpy as jnp
import numpy as np
from jax import lax
from jax.sharding import PartitionSpec as P

QUERY_HEADS = 32
KEY_HEADS = 16
HEAD_WIDTH = 64


def pair_tables(size):
    first_index, second_index = np.triu_indices(size)
    flat_index = (first_index * size + second_index).astype(np.int32)
    pair_weight = np.where(first_index == second_index, 1.0, math.sqrt(2.0)) / math.sqrt(size)
    return (flat_index, pair_weight)


def expand_single(vectors):
    size = vectors.shape[0]
    flat_index, pair_weight = pair_tables(size)
    widened = vectors.astype(jnp.float32)
    outer = (widened[:, None, :] * widened[None, :, :]).reshape(size * size, widened.shape[1])
    chosen = jnp.take(outer, jnp.asarray(flat_index), axis=0)
    return (chosen * jnp.asarray(pair_weight, jnp.float32)[:, None]).astype(jnp.bfloat16)


def expand_heads(turned):
    return lax.map(expand_single, turned)


def local(tokens, projection, context_state, norm_gain):
    group_total = QUERY_HEADS // KEY_HEADS
    local_heads = context_state.shape[0]
    projected = jnp.dot(
        lax.all_gather(tokens, "head", axis=0, tiled=True),
        projection,
        preferred_element_type=jnp.float32,
    ).astype(jnp.bfloat16)
    length = projected.shape[0]
    blocks = projected.reshape(length, local_heads, group_total + 2, HEAD_WIDTH)
    queries = blocks[:, :, :group_total]
    key_rows = blocks[:, :, group_total]
    values = blocks[:, :, group_total + 1]
    keys_turned = jnp.transpose(key_rows, (1, 2, 0))
    expanded_keys = expand_heads(keys_turned)
    block_state = jnp.einsum(
        "kfl,lkd->fkd", expanded_keys, values, preferred_element_type=jnp.float32
    )
    flattened = block_state.reshape(1, -1)
    pieces = lax.all_to_all(flattened, "ctx", split_axis=1, concat_axis=0, tiled=True)
    count = pieces.shape[0]
    strictly_lower = (
        lax.broadcasted_iota(jnp.int32, (count, count), 1)
        < lax.broadcasted_iota(jnp.int32, (count, count), 0)
    ).astype(jnp.float32)
    earlier_sum = jnp.dot(
        strictly_lower, pieces, precision=lax.Precision.HIGHEST, preferred_element_type=jnp.float32
    )
    earlier_sum = lax.all_to_all(
        earlier_sum, "ctx", split_axis=0, concat_axis=1, tiled=True
    ).reshape(block_state.shape)
    carried = jnp.transpose(context_state, (1, 0, 2))
    prefix = (carried + earlier_sum).astype(jnp.bfloat16)
    queries_turned = jnp.transpose(queries, (1, 2, 3, 0)).reshape(
        local_heads * group_total, HEAD_WIDTH, length
    )
    expanded_queries = expand_heads(queries_turned).reshape(local_heads, group_total, -1, length)
    carried_part = jnp.einsum(
        "kgfl,fkd->lkgd", expanded_queries, prefix, preferred_element_type=jnp.float32
    )
    scores = jnp.einsum("lkgd,mkd->kglm", queries, key_rows, preferred_element_type=jnp.float32)
    causal = lax.broadcasted_iota(jnp.int32, (length, length), 1) <= lax.broadcasted_iota(
        jnp.int32, (length, length), 0
    )
    scores = jnp.where(causal, scores * scores / HEAD_WIDTH, 0.0).astype(jnp.bfloat16)
    within = jnp.einsum("kglm,mkd->lkgd", scores, values, preferred_element_type=jnp.float32)
    combined = carried_part + within
    inverse_rms = lax.rsqrt(jnp.mean(combined * combined, -1, keepdims=True) + 1e-05)
    normed = combined * inverse_rms * norm_gain.reshape(local_heads, group_total, HEAD_WIDTH)
    normed = normed.astype(jnp.bfloat16).reshape(length, local_heads * group_total * HEAD_WIDTH)
    return lax.all_to_all(normed, "head", split_axis=0, concat_axis=1, tiled=True)


def solution(mesh):
    placed = (P(("ctx", "head"), None), P(None, "head"), P("head", None, None), P("head"))
    return jax.shard_map(
        local, mesh=mesh, in_specs=placed, out_specs=P(("ctx", "head"), None), check_vma=False
    )
```

profile of v0, /device:TPU:1, one launch (start us, length us, event | category | flops | bytes accessed | tf_op | source)
XLA Modules:
  0.0 340.3 jit_solution(15522484135481775688)
XLA Ops:
  6.5 0.7 all-gather.2.cloned.1.call-update
  7.3 0.0 copy-start.2
  7.3 0.0 copy-start.3
  7.3 40.9 %all-gather.2.cloned.1.call-done = bf16[1024,2048]{1,0:T(8,128)(2,1)} async-done(((bf16[128,2048]{1,0:T(8,128)(2,1)}), bf16[1024,2048]{1,0:T(8,128)(2,1)}) %all-gather.2.cloned.1.call-update) | async-done | bytes 4194320 | tf_op jit(solution)/shard_map/all_gather | solution.py:38
  48.2 4.6 %convolution_convert_fusion = bf16[1024,512]{0,1:T(8,128)(2,1)S(1)} fusion(bf16[1024,2048]{1,0:T(8,128)(2,1)} %all-gather.2.cloned.1.call-done, bf16[2048,512]{1,0:T(8,128)(2,1)S(1)} %copy-done), kind=kOutput, calls=%fused_computation.22 | convolution fusion | flops 2148007936 | bytes 7340032 | tf_op jit(solution)/shard_map/dot_general | solution.py:37
  52.7 1.0 copy-done.5
  53.8 60.9 %while.22 = (s32[]{:T(128)}, bf16[2,2080,1024]{2,1,0:T(8,128)(2,1)}, bf16[2,64,1024]{2,1,0:T(8,128)(2,1)S(1)}, s32[]{:T(128)}, s32[2080]{0:T(1024)S(1)}, /*index=5*/f32[2080]{0:T(1024)S(1)}) while((s32[]{:T(128)}, bf16[2,2080,1024]{2,1,0:T(8,128)(2,1)}, bf16[2,64,1024]{2,1,0:T(8,128)(2,1)S(1)}, s32[]{:T(128)}, ...), condition=%wide.region_1.0_spmd.clone, body=%wide.region_0.2_spmd.sunk.clone.sunk | while | flops 8522754 | bytes 47289288 | solution.py:31
  53.8 8.0 %broadcast_multiply_fusion.4 = f32[64,64,1024]{2,1,0:T(8,128)} fusion(f32[64,1024]{1,0:T(8,128)S(1)} %bitcast_convert_fusion.4), kind=kLoop, calls=%fused_computation.3.clone.1 | loop fusion | flops 4194304 | bytes 17039360 | tf_op jit(solution)/shard_map/while/body/eval_jaxpr/mul | solution.py:25
  61.9 16.4 %gather_fusion = f32[2080,1024]{1,0:T(8,128)} fusion(f32[4096,1024]{1,0:T(8,128)} %bitcast.90, s32[3072]{0:T(1024)S(1)} %pad_clamp_fusion.4), kind=kCustom, calls=%fused_computation.clone.clone.1 | custom fusion | bytes 17047680 | tf_op jit(solution)/shard_map/while/body/eval_jaxpr/jit(_take)/gather | solution.py:26
  78.3 5.9 %fusion.30 = bf16[2,2080,1024]{2,1,0:T(8,128)(2,1)} fusion(bf16[2,2080,1024]{2,1,0:T(8,128)(2,1)} %get-tuple-element.167, s32[]{:T(128)} %get-tuple-element.166, f32[2080,1024]{1,0:T(8,128)} %gather_fusion, f32[2080]{0:T(1024)S(1)} %get-tuple-element.177), kind=kLoop, calls=%fused_computation.5.clone.1 | loop fusion | flops 4259840 | bytes 12788352 | tf_op jit(solution)/shard_map/while/body/jit(dynamic_update_index_in_dim)/dynamic_update_slice | solution.py:31
  84.2 8.0 %broadcast_multiply_fusion.4 = f32[64,64,1024]{2,1,0:T(8,128)} fusion(f32[64,1024]{1,0:T(8,128)S(1)} %bitcast_convert_fusion.4), kind=kLoop, calls=%fused_computation.3.clone.1 | loop fusion | flops 4194304 | bytes 17039360 | tf_op jit(solution)/shard_map/while/body/eval_jaxpr/mul | solution.py:25
  92.3 16.4 %gather_fusion = f32[2080,1024]{1,0:T(8,128)} fusion(f32[4096,1024]{1,0:T(8,128)} %bitcast.90, s32[3072]{0:T(1024)S(1)} %pad_clamp_fusion.4), kind=kCustom, calls=%fused_computation.clone.clone.1 | custom fusion | bytes 17047680 | tf_op jit(solution)/shard_map/while/body/eval_jaxpr/jit(_take)/gather | solution.py:26
  108.7 5.9 %fusion.30 = bf16[2,2080,1024]{2,1,0:T(8,128)(2,1)} fusion(bf16[2,2080,1024]{2,1,0:T(8,128)(2,1)} %get-tuple-element.167, s32[]{:T(128)} %get-tuple-element.166, f32[2080,1024]{1,0:T(8,128)} %gather_fusion, f32[2080]{0:T(1024)S(1)} %get-tuple-element.177), kind=kLoop, calls=%fused_computation.5.clone.1 | loop fusion | flops 4259840 | bytes 12788352 | tf_op jit(solution)/shard_map/while/body/jit(dynamic_update_index_in_dim)/dynamic_update_slice | solution.py:31
  114.7 6.3 %convolution_bitcast_fusion.1 = f32[2080,2,64]{0,2,1:T(8,128)S(1)} fusion(bf16[2,2080,1024]{2,1,0:T(8,128)(2,1)} %get-tuple-element.60, bf16[1024,2,4,64]{0,3,2,1:T(8,128)(2,1)} %bitcast.98), kind=kOutput, calls=%fused_computation.18 | convolution fusion | flops 545259520 | bytes 9846784 | tf_op jit(solution)/shard_map/kfl,lkd->fkd/dot_general | solution.py:49
  121.0 2.4 copy.21
  123.4 4.3 %all_to_all.45 = f32[1,32,8320]{2,0,1:T(1,128)} reshape(f32[2080,2,64]{2,1,0:T(2,128)} %copy.21) | data formatting | bytes 2129920 | tf_op jit(solution)/shard_map/all_to_all | solution.py:53
  127.7 9.7 %all-to-all-start = ((f32[1,32,8320]{2,0,1:T(1,128)}), f32[1,32,8320]{2,0,1:T(1,128)S(1)}, u32[]{:S(2)}, u32[]{:S(2)}) async-start(f32[1,32,8320]{2,0,1:T(1,128)} %all_to_all.45), calls=%async_computation | async-start | bytes 2129920 | tf_op jit(solution)/shard_map/all_to_all | solution.py:53
  137.4 2.4 copy.19
  139.8 0.7 mul.81
  140.5 1.3 iota_compare_fusion
  141.8 1.1 slice.18
  142.8 21.7 %all-to-all-done = f32[1,32,8320]{2,0,1:T(1,128)S(1)} async-done(((f32[1,32,8320]{2,0,1:T(1,128)}), f32[1,32,8320]{2,0,1:T(1,128)S(1)}, u32[]{:S(2)}, u32[]{:S(2)}) %all-to-all-start) | async-done | bytes 1064992 | tf_op jit(solution)/shard_map/all_to_all | solution.py:53
  164.6 0.6 convolution_bitcast_fusion
  165.2 2.1 copy.23
  167.3 5.7 %all-to-all-start.1 = ((f32[32,1,8320]{2,1,0:T(1,128)}), f32[32,1,8320]{2,1,0:T(1,128)}, u32[]{:S(2)}, u32[]{:S(2)}) async-start(f32[32,1,8320]{2,1,0:T(1,128)} %copy.23), calls=%async_computation.1 | async-start | bytes 2129920 | tf_op jit(solution)/shard_map/all_to_all | solution.py:62
  173.1 121.7 %while.23 = (s32[]{:T(128)}, bf16[4,2080,1024]{2,1,0:T(8,128)(2,1)}, bf16[4,64,1024]{2,1,0:T(8,128)(2,1)S(1)}, s32[]{:T(128)}, s32[2080]{0:T(1024)S(1)}, /*index=5*/f32[2080]{0:T(1024)S(1)}) while((s32[]{:T(128)}, bf16[4,2080,1024]{2,1,0:T(8,128)(2,1)}, bf16[4,64,1024]{2,1,0:T(8,128)(2,1)S(1)}, s32[]{:T(128)}, ...), condition=%wide.region_3.5_spmd.clone, body=%wide.region_2.4_spmd.sunk.clone.sunk | while | flops 8522754 | bytes 47289288 | solution.py:31
  173.1 8.0 %broadcast_multiply_fusion.5 = f32[64,64,1024]{2,1,0:T(8,128)} fusion(f32[64,1024]{1,0:T(8,128)S(1)} %bitcast_convert_fusion.5), kind=kLoop, calls=%fused_computation.9.clone.1 | loop fusion | flops 4194304 | bytes 17039360 | tf_op jit(solution)/shard_map/while/body/eval_jaxpr/mul | solution.py:25
  181.1 16.4 %gather_fusion.1 = f32[2080,1024]{1,0:T(8,128)} fusion(f32[4096,1024]{1,0:T(8,128)} %bitcast.91, s32[3072]{0:T(1024)S(1)} %pad_clamp_fusion.5), kind=kCustom, calls=%fused_computation.1.clone.clone.1 | custom fusion | bytes 17047680 | tf_op jit(solution)/shard_map/while/body/eval_jaxpr/jit(_take)/gather | solution.py:26
  197.6 5.9 %fusion.31 = bf16[4,2080,1024]{2,1,0:T(8,128)(2,1)} fusion(bf16[4,2080,1024]{2,1,0:T(8,128)(2,1)} %get-tuple-element.149, s32[]{:T(128)} %get-tuple-element.148, f32[2080,1024]{1,0:T(8,128)} %gather_fusion.1, f32[2080]{0:T(1024)S(1)} %get-tuple-element.159), kind=kLoop, calls=%fused_computation.11.clone.1 | loop fusion | flops 4259840 | bytes 12788352 | tf_op jit(solution)/shard_map/while/body/jit(dynamic_update_index_in_dim)/dynamic_update_slice | solution.py:31
  203.5 8.0 %broadcast_multiply_fusion.5 = f32[64,64,1024]{2,1,0:T(8,128)} fusion(f32[64,1024]{1,0:T(8,128)S(1)} %bitcast_convert_fusion.5), kind=kLoop, calls=%fused_computation.9.clone.1 | loop fusion | flops 4194304 | bytes 17039360 | tf_op jit(solution)/shard_map/while/body/eval_jaxpr/mul | solution.py:25
  211.5 16.4 %gather_fusion.1 = f32[2080,1024]{1,0:T(8,128)} fusion(f32[4096,1024]{1,0:T(8,128)} %bitcast.91, s32[3072]{0:T(1024)S(1)} %pad_clamp_fusion.5), kind=kCustom, calls=%fused_computation.1.clone.clone.1 | custom fusion | bytes 17047680 | tf_op jit(solution)/shard_map/while/body/eval_jaxpr/jit(_take)/gather | solution.py:26
  228.0 5.9 %fusion.31 = bf16[4,2080,1024]{2,1,0:T(8,128)(2,1)} fusion(bf16[4,2080,1024]{2,1,0:T(8,128)(2,1)} %get-tuple-element.149, s32[]{:T(128)} %get-tuple-element.148, f32[2080,1024]{1,0:T(8,128)} %gather_fusion.1, f32[2080]{0:T(1024)S(1)} %get-tuple-element.159), kind=kLoop, calls=%fused_computation.11.clone.1 | loop fusion | flops 4259840 | bytes 12788352 | tf_op jit(solution)/shard_map/while/body/jit(dynamic_update_index_in_dim)/dynamic_update_slice | solution.py:31
  233.9 8.0 %broadcast_multiply_fusion.5 = f32[64,64,1024]{2,1,0:T(8,128)} fusion(f32[64,1024]{1,0:T(8,128)S(1)} %bitcast_convert_fusion.5), kind=kLoop, calls=%fused_computation.9.clone.1 | loop fusion | flops 4194304 | bytes 17039360 | tf_op jit(solution)/shard_map/while/body/eval_jaxpr/mul | solution.py:25
  242.0 16.4 %gather_fusion.1 = f32[2080,1024]{1,0:T(8,128)} fusion(f32[4096,1024]{1,0:T(8,128)} %bitcast.91, s32[3072]{0:T(1024)S(1)} %pad_clamp_fusion.5), kind=kCustom, calls=%fused_computation.1.clone.clone.1 | custom fusion | bytes 17047680 | tf_op jit(solution)/shard_map/while/body/eval_jaxpr/jit(_take)/gather | solution.py:26
  258.4 6.0 %fusion.31 = bf16[4,2080,1024]{2,1,0:T(8,128)(2,1)} fusion(bf16[4,2080,1024]{2,1,0:T(8,128)(2,1)} %get-tuple-element.149, s32[]{:T(128)} %get-tuple-element.148, f32[2080,1024]{1,0:T(8,128)} %gather_fusion.1, f32[2080]{0:T(1024)S(1)} %get-tuple-element.159), kind=kLoop, calls=%fused_computation.11.clone.1 | loop fusion | flops 4259840 | bytes 12788352 | tf_op jit(solution)/shard_map/while/body/jit(dynamic_update_index_in_dim)/dynamic_update_slice | solution.py:31
  264.4 8.0 %broadcast_multiply_fusion.5 = f32[64,64,1024]{2,1,0:T(8,128)} fusion(f32[64,1024]{1,0:T(8,128)S(1)} %bitcast_convert_fusion.5), kind=kLoop, calls=%fused_computation.9.clone.1 | loop fusion | flops 4194304 | bytes 17039360 | tf_op jit(solution)/shard_map/while/body/eval_jaxpr/mul | solution.py:25
  272.4 16.4 %gather_fusion.1 = f32[2080,1024]{1,0:T(8,128)} fusion(f32[4096,1024]{1,0:T(8,128)} %bitcast.91, s32[3072]{0:T(1024)S(1)} %pad_clamp_fusion.5), kind=kCustom, calls=%fused_computation.1.clone.clone.1 | custom fusion | bytes 17047680 | tf_op jit(solution)/shard_map/while/body/eval_jaxpr/jit(_take)/gather | solution.py:26
  288.9 5.9 %fusion.31 = bf16[4,2080,1024]{2,1,0:T(8,128)(2,1)} fusion(bf16[4,2080,1024]{2,1,0:T(8,128)(2,1)} %get-tuple-element.149, s32[]{:T(128)} %get-tuple-element.148, f32[2080,1024]{1,0:T(8,128)} %gather_fusion.1, f32[2080]{0:T(1024)S(1)} %get-tuple-element.159), kind=kLoop, calls=%fused_computation.11.clone.1 | loop fusion | flops 4259840 | bytes 12788352 | tf_op jit(solution)/shard_map/while/body/jit(dynamic_update_index_in_dim)/dynamic_update_slice | solution.py:31
  294.8 5.7 %fusion.5 = f32[2,64,2,1024]{3,1,2,0:T(8,128)S(1)} fusion(pred[1024,1024]{0,1:T(8,128)(4,1)} %iota_compare_fusion, bf16[1024,2,4,64]{0,3,2,1:T(8,128)(2,1)} %bitcast.100), kind=kOutput, calls=%fused_computation.19 | convolution fusion | flops 1090519040 | bytes 3145728 | tf_op jit(solution)/shard_map/kglm,mkd->lkgd/dot_general | solution.py:79
  300.4 3.8 %reduce = f32[32,8320]{1,0:T(8,128)S(1)} reduce(f32[32,1,8320]{2,1,0:T(1,128)} %all-to-all-done.1, f32[]{:T(128)} %constant.70), dimensions={1}, to_apply=%all_to_all.40.reduce_sub_computation | reduce | bytes 2129924 | tf_op jit(solution)/shard_map/all_to_all | solution.py:62
  304.2 2.6 reshape.71
  306.8 3.4 %fusion.8 = bf16[2080,2,64,1]{2,1,0,3:T(2,128)(2,1)S(1)} fusion(f32[2080,2,64]{2,1,0:T(2,128)} %reshape.71, f32[2,2080,64]{2,0,1:T(2,128)} %copy.19), kind=kLoop, calls=%fused_computation.25 | loop fusion | flops 532480 | bytes 2662400 | tf_op jit(solution)/shard_map/convert_element_type | solution.py:66
  310.3 7.8 %multiply_reduce_fusion = (f32[1024,2,2]{0,2,1:T(2,128)S(1)}, f32[1024,2,2,64]{0,3,2,1:T(8,128)S(1)}) fusion(f32[2,64,2,1024]{3,1,2,0:T(8,128)S(1)} %fusion.5, bf16[2,2,2080,1024]{3,2,1,0:T(8,128)(2,1)} %bitcast.92, bf16[2080,2,64,1]{2,1,0,3:T(2,128)(2,1)S(1)} %fusion.8), kind=kOutput, calls=%fused_computation.30 | convolution fusion | flops 1091301376 | bytes 19685376 | tf_op jit(solution)/shard_map/kgfl,fkd->lkgd/dot_general | solution.py:71
  318.1 0.1 multiply_convert_fusion.2
  318.2 0.1 copy.36
  318.3 0.1 copy.26
  318.4 14.0 %all_to_all.49 = bf16[8,128,256]{1,2,0:T(8,128)(2,1)S(1)} all-to-all(bf16[8,128,256]{1,2,0:T(8,128)(2,1)S(1)} %copy.26), channel_id=1, replica_groups=mesh['ctx'=32,'head'=8] {'head'}, dimensions={0} | all-to-all | bytes 1048576 | tf_op jit(solution)/shard_map/all_to_all | solution.py:84
  332.5 1.0 copy.27
  (31 shorter events, 0.2 us)
Async XLA Ops:
  6.5 41.6 %copy-start = (bf16[2048,512]{1,0:T(8,128)(2,1)S(1)}, bf16[2048,512]{1,0:T(8,128)(2,1)}, u32[]{:S(2)}) copy-start(bf16[2048,512]{1,0:T(8,128)(2,1)} %param.15) | copy-start | bytes 6291460
  6.5 41.6 %all-gather.2.cloned.1.call-start = ((), (), s32[]{:S(2)}) async-start(), calls=%async_computation.3 | async-start | bytes 4718592 | tf_op jit(solution)/shard_map/all_gather | solution.py:38
  7.3 46.5 %copy-start.2 = (s32[2080]{0:T(1024)S(1)}, s32[2080]{0:T(1024)}, u32[]{:S(2)}) copy-start(s32[2080]{0:T(1024)} %constant.97) | copy-start | bytes 24964
  7.3 46.5 %copy-start.3 = (f32[2080]{0:T(1024)S(1)}, f32[2080]{0:T(1024)}, u32[]{:S(2)}) copy-start(f32[2080]{0:T(1024)} %constant.47.clone..sunk.4) | copy-start | bytes 24964
  52.7 1.0 copy-start.5
  114.7 22.8 %copy-start.4 = (f32[2,2080,64]{1,2,0:T(8,128)S(1)}, f32[2,2080,64]{1,2,0:T(8,128)}, u32[]{:S(2)}) copy-start(f32[2,2080,64]{1,2,0:T(8,128)} %param.16) | copy-start | bytes 3194884
  114.7 25.2 %copy-start.7 = (f32[256]{0:T(256)S(1)}, f32[256]{0:T(256)}, u32[]{:S(2)}) copy-start(f32[256]{0:T(256)} %param.17) | copy-start | bytes 3076
  127.7 36.9 %all-to-all-start = ((f32[1,32,8320]{2,0,1:T(1,128)}), f32[1,32,8320]{2,0,1:T(1,128)S(1)}, u32[]{:S(2)}, u32[]{:S(2)}) async-start(f32[1,32,8320]{2,0,1:T(1,128)} %all_to_all.45), calls=%async_computation | async-start | bytes 2129920 | tf_op jit(solution)/shard_map/all_to_all | solution.py:53
  167.3 133.1 %all-to-all-start.1 = ((f32[32,1,8320]{2,1,0:T(1,128)}), f32[32,1,8320]{2,1,0:T(1,128)}, u32[]{:S(2)}, u32[]{:S(2)}) async-start(f32[32,1,8320]{2,1,0:T(1,128)} %copy.23), calls=%async_computation.1 | async-start | bytes 2129920 | tf_op jit(solution)/shard_map/all_to_all | solution.py:62
  310.3 7.8 %copy-start.6 = (f32[2,2,64]{2,1,0:T(2,128)S(1)}, f32[2,2,64]{2,1,0:T(2,128)}, u32[]{:S(2)}) copy-start(f32[2,2,64]{2,1,0:T(2,128)} %mul.81) | copy-start | bytes 3076
  310.3 23.2 %copy-start.1 = (bf16[2048,512]{1,0:T(8,128)(2,1)S(1)}, bf16[2048,512]{1,0:T(8,128)(2,1)}, u32[]{:S(2)}) copy-start(bf16[2048,512]{1,0:T(8,128)(2,1)} %param.15) | copy-start | bytes 6291460
Sparse Core Ops, SparseCore 0:
  9.2 38.8 all-gather.1
where the time goes:
time: 341 us; the launch traced here: 340 us
  local copies, waits for them, and re-layouts  117 us (34%)
  other arithmetic  92.4 us (27%)
  waiting for transfers between devices  63.3 us (19%)
  matrix products  24.9 us (7%)
  starting transfers between devices  15.5 us (5%)
  blocking collectives  14 us (4%)
  between operations  13.6 us (4%)
    gather x6, local copies, waits for them, and re-layouts, expand_single(): chosen = jnp.take(outer, jnp.asarray(flat_index), axis=0)  98.7 us
    mul x6, other arithmetic, expand_single(): widened[:, None, :] * widened[None, :, :]  48.1 us
    all_gather x1, waiting for transfers between devices, local(): lax.all_gather(tokens, 'head', axis=0, tiled=True)  40.9 us
    dynamic_update_slice x6, other arithmetic, expand_heads(): return lax.map(expand_single, turned)  35.6 us
    all_to_all x1, waiting for transfers between devices, local(): lax.all_to_all(flattened, 'ctx', split_axis=1, concat_axis=0, tiled=True)  21.7 us
    all_to_all x1, blocking collectives, local(): lax.all_to_all(normed, 'head', split_axis=0, concat_axis=1, tiled=True)  14 us
    all_to_all x1, starting transfers between devices, local(): lax.all_to_all(flattened, 'ctx', split_axis=1, concat_axis=0, tiled=True)  9.72 us
    dot_general x1, matrix products, local(): jnp.einsum('kgfl,fkd->lkgd', expanded_queries, prefix, preferred_element_...  7.78 us
  transfers between devices with their start and end apart: 3, of which 2 were waited for; matrix products, arithmetic and copies ran while one was open for 39% of the time, Pallas kernels for 0%

commit v1 on v0

v1 whole, which is shorter than its diff:
```python
import math

import jax
import jax.numpy as jnp
from jax import lax
from jax.experimental import pallas as pl
from jax.experimental.pallas import tpu as pltpu
from jax.sharding import PartitionSpec as P

MESH = pl.DeviceIdType.MESH
NZ, NX, NY = 8, 4, 4
WIDTH = 64
TOKENS = 1024
GROUP = 256
DEPTH = 2048
CHUNKS = 17
FEAT = 128 * CHUNKS
PIECE = 384
F32, BF16 = jnp.float32, jnp.bfloat16


def lanes(rows):
    return lax.broadcasted_iota(jnp.int32, (rows, 128), 1)


def left(value, amount):
    return pltpu.roll(value, 128 - amount, 1)


def write_features(twice, store):
    base = jnp.where(lanes(twice.shape[0]) < WIDTH, twice, left(twice, 16))
    for m in range(16):
        store(m, (base * left(twice, 17 + m)).astype(BF16))
    store(16, (twice * twice).astype(BF16))


def doubled(pair, half):
    low = lanes(pair.shape[0]) < WIDTH
    turned = pltpu.roll(pair, WIDTH, 1)
    return jnp.where(low, pair, turned) if half == 0 else jnp.where(low, turned, pair)


def kernel(tok_ref, w_hbm, ctx_hbm, gain_ref, out_ref,
           w_v, ctx_v, xall, q_v, kz_v, vk_v, phik, state, phiq, comb,
           square, ctx_f, ctx_t, xs, xr, zs, zr, es, er, ps, pt, ob,
           local_sem, gs, gr, xs_sem, xr_sem, zs_sem, zr_sem, es_sem, er_sem, ps_sem, pr_sem, os_sem, or_sem):
    me_ctx, me_head = lax.axis_index("ctx"), lax.axis_index("head")
    z, x = me_ctx // NX, me_ctx % NX
    y, core = me_head // 2, me_head % 2
    up, down, far = (y + 1) % NY, (y + NY - 1) % NY, (y + 2) % NY

    def head_partner(k):
        return (me_head + k) % (2 * NY)

    barrier = pltpu.get_barrier_semaphore()
    for k in range(1, 2 * NY):
        pl.semaphore_signal(barrier, inc=1, device_id=(me_ctx, head_partner(k)), device_id_type=MESH)
    for k in range(1, NX):
        pl.semaphore_signal(barrier, inc=1, device_id=(z * NX + (x + k) % NX, me_head), device_id_type=MESH)
    for k in range(1, NZ):
        pl.semaphore_signal(barrier, inc=1, device_id=(((z + k) % NZ) * NX + x, me_head), device_id_type=MESH)

    own = pltpu.make_async_copy(tok_ref, xall.at[me_head], local_sem.at[0])
    weights = pltpu.make_async_copy(w_hbm, w_v, local_sem.at[1])
    context = pltpu.make_async_copy(ctx_hbm, ctx_v, local_sem.at[2])
    own.start()
    weights.start()
    context.start()
    pl.semaphore_wait(barrier, 2 * NY - 1 + NX - 1 + NZ - 1)

    sent = []

    def send(src, dst, send_sem, recv_sem, device):
        copy = pltpu.make_async_remote_copy(
            src_ref=src, dst_ref=dst, send_sem=send_sem, recv_sem=recv_sem, device_id=device, device_id_type=MESH)
        copy.start()
        sent.append(copy)

    def arrived(dst, send_sem, recv_sem):
        pltpu.make_async_remote_copy(
            src_ref=dst, dst_ref=dst, send_sem=send_sem, recv_sem=recv_sem,
            device_id=(me_ctx, head_partner(1)), device_id_type=MESH).wait_recv()

    low, high = pl.ds(0, 64), pl.ds(64, 64)
    sib = (me_ctx, y * 2 + 1 - core)
    to_up, to_down = (me_ctx, up * 2 + core), (me_ctx, down * 2 + core)
    h_up, h_down, h_far = up * 2 + core, down * 2 + core, far * 2 + core
    s_up, s_down, s_far = up * 2 + 1 - core, down * 2 + 1 - core, far * 2 + 1 - core

    send(tok_ref.at[low], xall.at[me_head, low], gs.at[1], gr.at[1], to_up)
    send(tok_ref.at[high], xall.at[me_head, high], gs.at[2], gr.at[2], to_down)
    send(tok_ref, xall.at[me_head], gs.at[0], gr.at[0], sib)
    send(tok_ref.at[high], xall.at[me_head, high], gs.at[3], gr.at[3], to_up)
    send(tok_ref.at[low], xall.at[me_head, low], gs.at[4], gr.at[4], to_down)

    def pass_on(row, half, slot, device):
        send(xall.at[row, half], xall.at[row, half], gs.at[slot], gr.at[slot], device)

    def have(row, half, slot):
        arrived(xall.at[row, half], gs.at[slot], gr.at[slot])

    def project(group, first):
        rows = xall[pl.ds(2 * group, 2)].reshape(GROUP, DEPTH)
        made = jnp.dot(rows, w_v[...], preferred_element_type=F32).astype(BF16)
        for h in range(2):
            q_v[h, group] = made[:, 256 * h:256 * h + 128]
            pair = made[:, 256 * h + 128:256 * h + 256].astype(F32)
            kz_v[h, group] = jnp.where(lanes(GROUP) < WIDTH, pair, 0.0).astype(BF16)
            vk_v[h, group] = pltpu.roll(pair, WIDTH, 1).astype(BF16)
            twice = doubled(pair, 0)

            def store(m, value):
                phik[:, 128 * m:128 * m + 128] = value

            write_features(twice, store)
            values = pair.T[WIDTH:].astype(BF16)
            update = jnp.dot(values, phik[...], preferred_element_type=F32)
            if first:
                state[h] = update
            else:
                state[h] += update

    own.wait()
    weights.wait()
    arrived(xall.at[me_head], gs.at[0], gr.at[0])
    project(y, True)

    have(h_down, low, 1)
    pass_on(h_down, low, 5, to_up)
    pass_on(h_down, low, 7, sib)
    have(h_up, high, 2)
    pass_on(h_up, high, 6, to_down)
    pass_on(h_up, high, 8, sib)

    context.wait()
    start = 0
    for i in range(WIDTH):
        count = min(40, WIDTH - i)
        both = jnp.concatenate([ctx_v[0, start:start + count], ctx_v[1, start:start + count]], axis=1)
        square[129 * i:129 * i + count] = both
        start += WIDTH - i
    start = 0
    for i in range(WIDTH // 2):
        count = WIDTH // 2 - i
        both = jnp.concatenate(
            [ctx_v[0, start + 32:start + 32 + count], ctx_v[1, start + 32:start + 32 + count]], axis=1)
        square[pl.ds(128 * (i + 32) + 64 + i, count, 128)] = both
        start += WIDTH - i
    for apart in range(33):
        rows = square[pl.ds(apart, WIDTH, 129)]
        if apart == 0:
            ctx_f[2048:2112] = rows
            ctx_f[2112:2176] = jnp.zeros_like(rows)
        elif apart > 16:
            ctx_f[128 * (apart - 17):128 * (apart - 17) + 64] = rows
        else:
            at = 128 * (apart - 1) + 64
            ctx_f[at:at + 48] = rows[16:]
            ctx_f[at + 48:at + 64] = rows[:16]
    feature = lax.broadcasted_iota(jnp.int32, (1, FEAT), 1)
    in_second = (feature % 128) >= WIDTH
    diagonal = (feature >= 2048) & (feature < 2112)
    unused = feature >= 2112
    twin = (feature >= 15 * 128) & (feature < 15 * 128 + 64)
    square_weight = jnp.where(unused, 0.0, jnp.where(diagonal | twin, 1.0 / 64, 2.0 / 64)).astype(F32)
    single_weight = jnp.where(
        unused, 0.0, jnp.where(diagonal, 1.0 / 8, jnp.where(twin, math.sqrt(2.0) / 16, math.sqrt(2.0) / 8))).astype(F32)
    for m in range(CHUNKS):
        turned = ctx_f[128 * m:128 * m + 128].T
        ctx_t[:, :, 128 * m:128 * m + 128] = turned.reshape(8, 16, 128)

    have(h_down, high, 3)
    pass_on(h_down, high, 9, sib)
    have(h_up, low, 4)
    pass_on(h_up, low, 10, sib)
    have(s_down, low, 7)
    have(s_down, high, 9)
    project(down, False)
    have(s_up, high, 8)
    have(s_up, low, 10)
    project(up, False)
    have(h_far, low, 5)
    pass_on(h_far, low, 11, sib)
    have(h_far, high, 6)
    pass_on(h_far, high, 12, sib)
    have(s_far, low, 11)
    have(s_far, high, 12)
    project(far, False)

    def x_out(h):
        xs[h] = state[h].reshape(NX, 16, FEAT).astype(BF16)
        xr[h, x] = xs[h, x]
        for k in range(1, NX):
            there = (x + k) % NX
            send(xs.at[h, there], xr.at[h, x], xs_sem.at[h, k], xr_sem.at[h, k], (z * NX + there, me_head))

    def x_in(h):
        for k in range(1, NX):
            arrived(xr.at[h, (x + NX - k) % NX], xs_sem.at[h, k], xr_sem.at[h, k])
        total = xr[h, 0].astype(F32)
        for k in range(1, NX):
            total += xr[h, k].astype(F32)
        total = total.astype(BF16)
        for k in range(NZ):
            zs[h, k] = total[:, 256 * k:256 * k + PIECE]
        zr[h, z] = zs[h, z]
        for k in range(1, NZ):
            there = (z + k) % NZ
            send(zs.at[h, there], zr.at[h, z], zs_sem.at[h, k], zr_sem.at[h, k], (there * NX + x, me_head))

    def z_in(h):
        for k in range(1, NZ):
            arrived(zr.at[h, (z + NZ - k) % NZ], zs_sem.at[h, k], zr_sem.at[h, k])
        running = jnp.zeros((16, PIECE), F32)
        for k in range(NZ):
            es[h, k] = running.astype(BF16)
            running += zr[h, k].astype(F32)
        er[h, z] = es[h, z]
        for k in range(1, NZ):
            there = (z + k) % NZ
            send(es.at[h, there], er.at[h, z], es_sem.at[h, k], er_sem.at[h, k], (there * NX + x, me_head))

    def e_in(h):
        for k in range(1, NZ):
            arrived(er.at[h, (z + NZ - k) % NZ], es_sem.at[h, k], er_sem.at[h, k])
        earlier = jnp.concatenate(
            [er[h, k, :, :256] for k in range(NZ - 1)] + [er[h, NZ - 1]], axis=1).astype(F32)
        before = ctx_t[4 * h + x] * single_weight
        running = earlier
        for k in range(NX):
            ps[h, k] = (before + running * square_weight).astype(BF16)
            if k < NX - 1:
                running += xr[h, k].astype(F32)
        pt[h, x] = ps[h, x]
        for k in range(1, NX):
            there = (x + k) % NX
            send(ps.at[h, there], pt.at[h, x], ps_sem.at[h, k], pr_sem.at[h, k], (z * NX + there, me_head))

    causal = (lax.broadcasted_iota(jnp.int32, (GROUP, GROUP), 1)
              <= lax.broadcasted_iota(jnp.int32, (GROUP, GROUP), 0))

    def tile(h, i):
        pair = q_v[h, i].astype(F32)
        for g in range(2):
            twice = doubled(pair, g)

            def store(m, value):
                phiq[h, i, g, :, 128 * m:128 * m + 128] = value

            write_features(twice, store)
            query = twice.astype(BF16)
            total = None
            for j in range(i + 1):
                score = lax.dot_general(
                    query, kz_v[h, j], (((1,), (1,)), ((), ())), preferred_element_type=F32)
                score = score * score * (1.0 / WIDTH)
                if j == i:
                    score = jnp.where(causal, score, 0.0)
                part = jnp.dot(score.astype(BF16), vk_v[h, j], preferred_element_type=F32)
                total = part if total is None else total + part
            comb[h, i, g] = total

    def finish(h):
        for k in range(1, NX):
            arrived(pt.at[h, (x + NX - k) % NX], ps_sem.at[h, k], pr_sem.at[h, k])
        prefix = pt[h].reshape(WIDTH, FEAT)

        def one(i, carry):
            made = []
            for g in range(2):
                carried = lax.dot_general(
                    phiq[h, i, g], prefix, (((1,), (1,)), ((), ())), preferred_element_type=F32)
                combined = carried + comb[h, i, g][:, :WIDTH]
                inverse = lax.rsqrt(jnp.mean(combined * combined, -1, keepdims=True) + 1e-05)
                made.append(combined * inverse)
            both = jnp.concatenate(made, axis=1) * gain_ref[:, 128 * h:128 * h + 128]
            ob[h, pl.ds(2 * i, 2)] = both.astype(BF16).reshape(2, 128, 128)
            return carry

        lax.fori_loop(0, TOKENS // GROUP, one, 0)
        place = pl.ds(pl.multiple_of(me_head * 256 + 128 * h, 128), 128)
        for k in range(1, 2 * NY):
            there = head_partner(k)
            send(ob.at[h, there], out_ref.at[:, place], os_sem.at[h, k], or_sem.at[h, k], (me_ctx, there))
        return pltpu.make_async_copy(ob.at[h, me_head], out_ref.at[:, place], local_sem.at[3 + h])

    x_out(0)
    x_out(1)
    tile(0, 0)
    tile(0, 1)
    tile(0, 2)
    x_in(0)
    tile(0, 3)
    x_in(1)
    tile(1, 0)
    tile(1, 1)
    z_in(0)
    tile(1, 2)
    z_in(1)
    tile(1, 3)
    e_in(0)
    e_in(1)
    last = []
    for h in range(2):
        copy = finish(h)
        copy.start()
        last.append(copy)
    for copy in last:
        copy.wait()
    for h in range(2):
        for k in range(1, 2 * NY):
            there = (me_head + 2 * NY - k) % (2 * NY)
            place = pl.ds(pl.multiple_of(there * 256 + 128 * h, 128), 128)
            arrived(out_ref.at[:, place], os_sem.at[h, k], or_sem.at[h, k])
    for copy in sent:
        copy.wait_send()


def local(tokens, projection, context_state, norm_gain):
    dma = pltpu.SemaphoreType.DMA
    return pl.pallas_call(
        kernel,
        out_shape=jax.ShapeDtypeStruct((128, 2048), BF16),
        in_specs=[pl.BlockSpec(memory_space=pl.ANY)] * 3 + [pl.BlockSpec(memory_space=pltpu.VMEM)],
        out_specs=pl.BlockSpec(memory_space=pl.ANY),
        scratch_shapes=[
            pltpu.VMEM((DEPTH, 512), BF16),
            pltpu.VMEM((2, 2080, WIDTH), F32),
            pltpu.VMEM((2 * NY, 128, DEPTH), BF16),
            pltpu.VMEM((2, 4, GROUP, 128), BF16),
            pltpu.VMEM((2, 4, GROUP, 128), BF16),
            pltpu.VMEM((2, 4, GROUP, 128), BF16),
            pltpu.VMEM((GROUP, FEAT), BF16),
            pltpu.VMEM((2, WIDTH, FEAT), F32),
            pltpu.VMEM((2, 4, 2, GROUP, FEAT), BF16),
            pltpu.VMEM((2, 4, 2, GROUP, 128), F32),
            pltpu.VMEM((64 * 129 + 8, 128), F32),
            pltpu.VMEM((FEAT, 128), F32),
            pltpu.VMEM((8, 16, FEAT), F32),
            pltpu.VMEM((2, NX, 16, FEAT), BF16),
            pltpu.VMEM((2, NX, 16, FEAT), BF16),
            pltpu.VMEM((2, NZ, 16, PIECE), BF16),
            pltpu.VMEM((2, NZ, 16, PIECE), BF16),
            pltpu.VMEM((2, NZ, 16, PIECE), BF16),
            pltpu.VMEM((2, NZ, 16, PIECE), BF16),
            pltpu.VMEM((2, NX, 16, FEAT), BF16),
            pltpu.VMEM((2, NX, 16, FEAT), BF16),
            pltpu.VMEM((2, 2 * NY, 128, 128), BF16),
            dma((5,)),
            dma((13,)),
            dma((13,)),
            dma((2, NX)),
            dma((2, NX)),
            dma((2, NZ)),
            dma((2, NZ)),
            dma((2, NZ)),
            dma((2, NZ)),
            dma((2, NX)),
            dma((2, NX)),
            dma((2, 2 * NY)),
            dma((2, 2 * NY)),
        ],
        compiler_params=pltpu.CompilerParams(
            collective_id=0, has_side_effects=True, vmem_limit_bytes=58 * 2**20),
        cost_estimate=pl.CostEstimate(flops=10 * 10**9, bytes_accessed=8 * 2**20, transcendentals=0),
    )(tokens, projection, context_state, norm_gain.reshape(1, -1))


def solution(mesh):
    placed = (P(("ctx", "head"), None), P(None, "head"), P("head", None, None), P("head"))
    return jax.shard_map(
        local, mesh=mesh, in_specs=placed, out_specs=P(("ctx", "head"), None), check_vma=False
    )
```

time: 341 us -> 75.2 us (0.22)
  local copies, waits for them, and re-layouts: 117 us -> 4.67 us
  other arithmetic: 92.4 us -> 0 us
  Pallas kernels: 0 us -> 70.4 us
  waiting for transfers between devices: 63.3 us -> 0 us
  matrix products: 24.9 us -> 0 us
  starting transfers between devices: 15.5 us -> 0 us
  blocking collectives: 14 us -> 0 us
  between operations: 13.6 us -> 0.01 us
    gather x6 -> x0, local copies, waits for them, and re-layouts: 98.7 us -> none  [expand_single(): chosen = jnp.take(outer, jnp.asarray(flat_index), axis=0)]
    pallas_call x0 -> x1, Pallas kernels: none -> 70.4 us  [local(): pl.pallas_call(kernel, out_shape=jax.ShapeDtypeStruct((128, 2048), BF16),...]
    mul x6 -> x0, other arithmetic: 48.1 us -> none  [expand_single(): widened[:, None, :] * widened[None, :, :]]
    all_gather x1 -> x0, waiting for transfers between devices: 40.9 us -> none  [local(): lax.all_gather(tokens, 'head', axis=0, tiled=True)]
    dynamic_update_slice x6 -> x0, other arithmetic: 35.6 us -> none  [expand_heads(): return lax.map(expand_single, turned)]
    dot_general x5 -> x0, matrix products: 24.9 us -> none  [the longest x1 7.78 us: local(): jnp.einsum('kgfl,fkd->lkgd', expanded_queries, prefix, preferred_element_...]
    all_to_all x2 -> x0, waiting for transfers between devices: 21.7 us -> none  [the longest x1 21.7 us: local(): lax.all_to_all(flattened, 'ctx', split_axis=1, concat_axis=0, tiled=True)]
    all_to_all x2 -> x0, starting transfers between devices: 15.5 us -> none  [the longest x1 9.72 us: local(): lax.all_to_all(flattened, 'ctx', split_axis=1, concat_axis=0, tiled=True)]
  transfers between devices with their start and end apart: 3 -> 0, of which waited for: 2 -> 0; matrix products, arithmetic and copies ran while one was open for 39% -> 0% of each run, Pallas kernels for 0% -> 0%
where the time goes in v1:
time: 75.2 us; the launch traced here: 75.1 us
  Pallas kernels  70.4 us (94%)
  local copies, waits for them, and re-layouts  4.67 us (6%)
    pallas_call x1, Pallas kernels, local(): pl.pallas_call(kernel, out_shape=jax.ShapeDtypeStruct((128, 2048), BF16),...  70.4 us
    unnamed x2, local copies, waits for them, and re-layouts  4.67 us

profile of v1, /device:TPU:1, one launch (start us, length us, event | category | flops | bytes accessed | tf_op | source)
XLA Modules:
  0.0 75.1 jit_solution(10379498200170001321)
XLA Ops:
  0.0 2.8 %copy.5.ctx_hbm = f32[2,2080,64]{2,1,0:T(8,128)} copy(f32[2,2080,64]{1,2,0:T(8,128)} %param.6) | data formatting | bytes 2129920 | tf_op args[2]
  2.8 70.4 %shard_map.46 = bf16[128,2048]{1,0:T(8,128)(2,1)} custom-call(bf16[128,2048]{1,0:T(8,128)(2,1)} %tok_ref.1, bf16[2048,512]{1,0:T(8,128)(2,1)} %w_hbm.1, f32[2,2080,64]{2,1,0:T(8,128)} %copy.5.ctx_hbm, f32[1,256]{1,0:T(1,128)} %bitcast.1), custom_call_target="tpu_custom_call" | custom-call | flops 10000000000 | bytes 8388608 | tf_op jit(solution)/shard_map/pallas_call | solution.py:321
  73.2 1.9 %copy.7 = bf16[128,2048]{1,0:T(8,128)(2,1)} copy(bf16[128,2048]{1,0:T(8,128)(2,1)} %shard_map.46) | data formatting | bytes 1048576

commit v2 on v1

--- a/solution.py
+++ b/solution.py
@@ -1,3 +1,4 @@
+import functools
 import math
 
 import jax
@@ -15,6 +16,7 @@
 DEPTH = 2048
 CHUNKS = 17
 FEAT = 128 * CHUNKS
+PAIRS = 2080
 PIECE = 384
 F32, BF16 = jnp.float32, jnp.bfloat16
 
@@ -41,9 +43,9 @@
 
 
 def kernel(tok_ref, w_hbm, ctx_hbm, gain_ref, out_ref,
-           w_v, ctx_v, xall, q_v, kz_v, vk_v, phik, state, phiq, comb,
-           square, ctx_f, ctx_t, xs, xr, zs, zr, es, er, ps, pt, ob,
-           local_sem, gs, gr, xs_sem, xr_sem, zs_sem, zr_sem, es_sem, er_sem, ps_sem, pr_sem, os_sem, or_sem):
+           w_v, ctx_v, xall, q_v, kz_v, vk_v, kv_v, phik, state, phiq, comb,
+           square, ctx_f, ctx_t, xs, xr, zs, zr, es, er, tails, ps, pt, turned, ob,
+           met, local_sem, gs, gr, xs_sem, xr_sem, zs_sem, zr_sem, es_sem, er_sem, ps_sem, pr_sem, os_sem, or_sem):
     me_ctx, me_head = lax.axis_index("ctx"), lax.axis_index("head")
     z, x = me_ctx // NX, me_ctx % NX
     y, core = me_head // 2, me_head % 2
@@ -53,20 +55,42 @@
         return (me_head + k) % (2 * NY)
 
     barrier = pltpu.get_barrier_semaphore()
-    for k in range(1, 2 * NY):
-        pl.semaphore_signal(barrier, inc=1, device_id=(me_ctx, head_partner(k)), device_id_type=MESH)
+    sib = (me_ctx, y * 2 + 1 - core)
+    for other in (up, down):
+        pl.semaphore_signal(barrier, inc=1, device_id=(me_ctx, other * 2), device_id_type=MESH)
+
+    @pl.when(core == 1)
+    def _():
+        pl.semaphore_signal(barrier, inc=1, device_id=sib, device_id_type=MESH)
+
     for k in range(1, NX):
-        pl.semaphore_signal(barrier, inc=1, device_id=(z * NX + (x + k) % NX, me_head), device_id_type=MESH)
+        pl.semaphore_signal(barrier, inc=1, device_id=(z * NX + (x + k) % NX, y * 2 + 1), device_id_type=MESH)
     for k in range(1, NZ):
-        pl.semaphore_signal(barrier, inc=1, device_id=(((z + k) % NZ) * NX + x, me_head), device_id_type=MESH)
+        pl.semaphore_signal(barrier, inc=1, device_id=(((z + k) % NZ) * NX + x, y * 2 + 1), device_id_type=MESH)
 
     own = pltpu.make_async_copy(tok_ref, xall.at[me_head], local_sem.at[0])
-    weights = pltpu.make_async_copy(w_hbm, w_v, local_sem.at[1])
+    weights = []
+    for n, at in enumerate((128, 384, 0, 256)):
+        weights.append(pltpu.make_async_copy(
+            w_hbm.at[:, at:at + 128], w_v.at[n // 2, :, 128 * (n % 2):128 * (n % 2) + 128], local_sem.at[5 + n]))
     context = pltpu.make_async_copy(ctx_hbm, ctx_v, local_sem.at[2])
     own.start()
-    weights.start()
+    for part in weights:
+        part.start()
     context.start()
-    pl.semaphore_wait(barrier, 2 * NY - 1 + NX - 1 + NZ - 1)
+
+    @pl.when(core == 0)
+    def _():
+        pl.semaphore_wait(barrier, 5)
+        pl.semaphore_signal(met.at[0], inc=1, device_id=sib, device_id_type=MESH)
+
+    @pl.when(core == 1)
+    def _():
+        pl.semaphore_wait(met.at[0], 1)
+
+
+    def stage(work):
+        pl.when(me_head >= 0)(work)
 
     sent = []
 
@@ -82,7 +106,6 @@
             device_id=(me_ctx, head_partner(1)), device_id_type=MESH).wait_recv()
 
     low, high = pl.ds(0, 64), pl.ds(64, 64)
-    sib = (me_ctx, y * 2 + 1 - core)
     to_up, to_down = (me_ctx, up * 2 + core), (me_ctx, down * 2 + core)
     h_up, h_down, h_far = up * 2 + core, down * 2 + core, far * 2 + core
     s_up, s_down, s_far = up * 2 + 1 - core, down * 2 + 1 - core, far * 2 + 1 - core
@@ -99,29 +122,49 @@
     def have(row, half, slot):
         arrived(xall.at[row, half], gs.at[slot], gr.at[slot])
 
-    def project(group, first):
-        rows = xall[pl.ds(2 * group, 2)].reshape(GROUP, DEPTH)
-        made = jnp.dot(rows, w_v[...], preferred_element_type=F32).astype(BF16)
+    def project(group, first=False, then=None):
+        def rows():
+            return xall[pl.ds(2 * group, 2)].reshape(GROUP, DEPTH)
+
+        @stage
+        def _():
+            made = jnp.dot(rows(), w_v[0], preferred_element_type=F32).astype(BF16).astype(F32)
+            for h in range(2):
+                kv_v[h] = made[:, 128 * h:128 * h + 128]
+
         for h in range(2):
-            q_v[h, group] = made[:, 256 * h:256 * h + 128]
-            pair = made[:, 256 * h + 128:256 * h + 256].astype(F32)
-            kz_v[h, group] = jnp.where(lanes(GROUP) < WIDTH, pair, 0.0).astype(BF16)
-            vk_v[h, group] = pltpu.roll(pair, WIDTH, 1).astype(BF16)
-            twice = doubled(pair, 0)
-
-            def store(m, value):
-                phik[:, 128 * m:128 * m + 128] = value
-
-            write_features(twice, store)
-            values = pair.T[WIDTH:].astype(BF16)
-            update = jnp.dot(values, phik[...], preferred_element_type=F32)
-            if first:
-                state[h] = update
-            else:
-                state[h] += update
+            @stage
+            def _():
+                pair = kv_v[h]
+                twice = doubled(pair, 0)
+
+                def store(m, value):
+                    phik[:, 128 * m:128 * m + 128] = value
+
+                write_features(twice, store)
+                values = pair.T[WIDTH:].astype(BF16)
+                update = jnp.dot(values, phik[...], preferred_element_type=F32)
+                if first:
+                    state[h] = update
+                else:
+                    state[h] += update
+
+            if then is not None:
+                then(h)
+
+        @stage
+        def _():
+            for h in range(2):
+                pair = kv_v[h]
+                kz_v[h, group] = jnp.where(lanes(GROUP) < WIDTH, pair, 0.0).astype(BF16)
+                vk_v[h, group] = pltpu.roll(pair, WIDTH, 1).astype(BF16)
+            made = jnp.dot(rows(), w_v[1], preferred_element_type=F32).astype(BF16)
+            for h in range(2):
+                q_v[h, group] = made[:, 128 * h:128 * h + 128]
 
     own.wait()
-    weights.wait()
+    for part in weights:
+        part.wait()
     arrived(xall.at[me_head], gs.at[0], gr.at[0])
     project(y, True)
 
@@ -133,18 +176,18 @@
     pass_on(h_up, high, 8, sib)
 
     context.wait()
+    for at in range(0, PAIRS, 128):
+        end = min(at + 128, PAIRS)
+        ctx_f[at:end] = ctx_v[:, at:end].T
     start = 0
     for i in range(WIDTH):
         count = min(40, WIDTH - i)
-        both = jnp.concatenate([ctx_v[0, start:start + count], ctx_v[1, start:start + count]], axis=1)
-        square[129 * i:129 * i + count] = both
+        square[129 * i:129 * i + count] = ctx_f[start:start + count]
         start += WIDTH - i
     start = 0
     for i in range(WIDTH // 2):
         count = WIDTH // 2 - i
-        both = jnp.concatenate(
-            [ctx_v[0, start + 32:start + 32 + count], ctx_v[1, start + 32:start + 32 + count]], axis=1)
-        square[pl.ds(128 * (i + 32) + 64 + i, count, 128)] = both
+        square[pl.ds(128 * (i + 32) + 64 + i, count, 128)] = ctx_f[start + 32:start + 32 + count]
         start += WIDTH - i
     for apart in range(33):
         rows = square[pl.ds(apart, WIDTH, 129)]
@@ -166,8 +209,8 @@
     single_weight = jnp.where(
         unused, 0.0, jnp.where(diagonal, 1.0 / 8, jnp.where(twin, math.sqrt(2.0) / 16, math.sqrt(2.0) / 8))).astype(F32)
     for m in range(CHUNKS):
-        turned = ctx_f[128 * m:128 * m + 128].T
-        ctx_t[:, :, 128 * m:128 * m + 128] = turned.reshape(8, 16, 128)
+        rows = ctx_f[128 * m:128 * m + 128].T
+        ctx_t[:, :, 128 * m:128 * m + 128] = rows.reshape(8, 16, 128)
 
     have(h_down, high, 3)
     pass_on(h_down, high, 9, sib)
@@ -175,17 +218,16 @@
     pass_on(h_up, low, 10, sib)
     have(s_down, low, 7)
     have(s_down, high, 9)
-    project(down, False)
+    project(down)
     have(s_up, high, 8)
     have(s_up, low, 10)
-    project(up, False)
+    project(up)
     have(h_far, low, 5)
     pass_on(h_far, low, 11, sib)
     have(h_far, high, 6)
     pass_on(h_far, high, 12, sib)
     have(s_far, low, 11)
     have(s_far, high, 12)
-    project(far, False)
 
     def x_out(h):
         xs[h] = state[h].reshape(NX, 16, FEAT).astype(BF16)
@@ -202,7 +244,7 @@
             total += xr[h, k].astype(F32)
         total = total.astype(BF16)
         for k in range(NZ):
-            zs[h, k] = total[:, 256 * k:256 * k + PIECE]
+            zs[h, k] = jnp.concatenate([total[:, 256 * k:256 * k + 256], total[:, 2048:]], axis=1)
         zr[h, z] = zs[h, z]
         for k in range(1, NZ):
             there = (z + k) % NZ
@@ -211,10 +253,13 @@
     def z_in(h):
         for k in range(1, NZ):
             arrived(zr.at[h, (z + NZ - k) % NZ], zs_sem.at[h, k], zr_sem.at[h, k])
-        running = jnp.zeros((16, PIECE), F32)
+        running = jnp.zeros((16, 256), F32)
+        tail = jnp.zeros((16, 128), F32)
         for k in range(NZ):
             es[h, k] = running.astype(BF16)
-            running += zr[h, k].astype(F32)
+            running += zr[h, k, :, :256].astype(F32)
+            tail += jnp.where(k < z, zr[h, k, :, 256:].astype(F32), 0.0)
+        tails[h] = tail
         er[h, z] = es[h, z]
         for k in range(1, NZ):
             there = (z + k) % NZ
@@ -224,7 +269,7 @@
         for k in range(1, NZ):
             arrived(er.at[h, (z + NZ - k) % NZ], es_sem.at[h, k], er_sem.at[h, k])
         earlier = jnp.concatenate(
-            [er[h, k, :, :256] for k in range(NZ - 1)] + [er[h, NZ - 1]], axis=1).astype(F32)
+            [er[h, k].astype(F32) for k in range(NZ)] + [tails[h]], axis=1)
         before = ctx_t[4 * h + x] * single_weight
         running = earlier
         for k in range(NX):
@@ -260,76 +305,88 @@
                 total = part if total is None else total + part
             comb[h, i, g] = total
 
+    kept = []
+
     def finish(h):
         for k in range(1, NX):
             arrived(pt.at[h, (x + NX - k) % NX], ps_sem.at[h, k], pr_sem.at[h, k])
-        prefix = pt[h].reshape(WIDTH, FEAT)
-
-        def one(i, carry):
-            made = []
-            for g in range(2):
-                carried = lax.dot_general(
-                    phiq[h, i, g], prefix, (((1,), (1,)), ((), ())), preferred_element_type=F32)
-                combined = carried + comb[h, i, g][:, :WIDTH]
+        turned[h] = pt[h].reshape(WIDTH, FEAT).astype(F32).T.astype(BF16)
+        for k in (2, 1, 3, 0):
+            i = (y + k) % NY
+
+            @stage
+            def _():
+                carried = jnp.dot(
+                    phiq[h, i].reshape(2 * GROUP, FEAT), turned[h], preferred_element_type=F32)
+                combined = carried + comb[h, i].reshape(2 * GROUP, 128)[:, :WIDTH]
                 inverse = lax.rsqrt(jnp.mean(combined * combined, -1, keepdims=True) + 1e-05)
-                made.append(combined * inverse)
-            both = jnp.concatenate(made, axis=1) * gain_ref[:, 128 * h:128 * h + 128]
-            ob[h, pl.ds(2 * i, 2)] = both.astype(BF16).reshape(2, 128, 128)
-            return carry
-
-        lax.fori_loop(0, TOKENS // GROUP, one, 0)
-        place = pl.ds(pl.multiple_of(me_head * 256 + 128 * h, 128), 128)
-        for k in range(1, 2 * NY):
-            there = head_partner(k)
-            send(ob.at[h, there], out_ref.at[:, place], os_sem.at[h, k], or_sem.at[h, k], (me_ctx, there))
-        return pltpu.make_async_copy(ob.at[h, me_head], out_ref.at[:, place], local_sem.at[3 + h])
-
-    x_out(0)
-    x_out(1)
-    tile(0, 0)
-    tile(0, 1)
-    tile(0, 2)
+                made = combined * inverse
+                both = jnp.concatenate([made[:GROUP], made[GROUP:]], axis=1) * gain_ref[:, 128 * h:128 * h + 128]
+                ob[h, pl.ds(2 * i, 2)] = both.astype(BF16).reshape(2, 128, 128)
+
+            for d in range(2):
+                there = i * 2 + (core + d) % 2
+                if k == 0 and d == 0:
+                    copy = pltpu.make_async_copy(ob.at[h, there], out_ref.at[2 * me_head + h], local_sem.at[3 + h])
+                    copy.start()
+                    kept.append(copy)
+                else:
+                    send(ob.at[h, there], out_ref.at[2 * me_head + h],
+                         os_sem.at[h, 2 * k + d], or_sem.at[h, 2 * k + d], (me_ctx, there))
+
+    @pl.when(core == 1)
+    def _():
+        pl.semaphore_wait(barrier, 2 * (NX - 1 + NZ - 1))
+        pl.semaphore_signal(met.at[1], inc=1, device_id=sib, device_id_type=MESH)
+
+    @pl.when(core == 0)
+    def _():
+        pl.semaphore_wait(met.at[1], 1)
+
+    project(far, then=x_out)
+    stage(functools.partial(tile, 0, 0))
+    stage(functools.partial(tile, 0, 1))
+    stage(functools.partial(tile, 0, 2))
     x_in(0)
-    tile(0, 3)
+    stage(functools.partial(tile, 0, 3))
     x_in(1)
-    tile(1, 0)
-    tile(1, 1)
+    stage(functools.partial(tile, 1, 0))
+    stage(functools.partial(tile, 1, 1))
     z_in(0)
-    tile(1, 2)
+    stage(functools.partial(tile, 1, 2))
     z_in(1)
-    tile(1, 3)
+    stage(functools.partial(tile, 1, 3))
     e_in(0)
     e_in(1)
-    last = []
-    for h in range(2):
-        copy = finish(h)
-        copy.start()
-        last.append(copy)
-    for copy in last:
+    finish(0)
+    finish(1)
+    for copy in kept:
         copy.wait()
     for h in range(2):
-        for k in range(1, 2 * NY):
-            there = (me_head + 2 * NY - k) % (2 * NY)
-            place = pl.ds(pl.multiple_of(there * 256 + 128 * h, 128), 128)
-            arrived(out_ref.at[:, place], os_sem.at[h, k], or_sem.at[h, k])
+        for k in range(NY):
+            for d in range(2):
+                if k + d > 0:
+                    there = ((y + NY - k) % NY) * 2 + (core + d) % 2
+                    arrived(out_ref.at[2 * there + h], os_sem.at[h, 2 * k + d], or_sem.at[h, 2 * k + d])
     for copy in sent:
         copy.wait_send()
 
 
 def local(tokens, projection, context_state, norm_gain):
     dma = pltpu.SemaphoreType.DMA
-    return pl.pallas_call(
+    pieces = pl.pallas_call(
         kernel,
-        out_shape=jax.ShapeDtypeStruct((128, 2048), BF16),
+        out_shape=jax.ShapeDtypeStruct((4 * NY, 128, 128), BF16),
         in_specs=[pl.BlockSpec(memory_space=pl.ANY)] * 3 + [pl.BlockSpec(memory_space=pltpu.VMEM)],
         out_specs=pl.BlockSpec(memory_space=pl.ANY),
         scratch_shapes=[
-            pltpu.VMEM((DEPTH, 512), BF16),
-            pltpu.VMEM((2, 2080, WIDTH), F32),
+            pltpu.VMEM((2, DEPTH, 256), BF16),
+            pltpu.VMEM((128, PAIRS), F32),
             pltpu.VMEM((2 * NY, 128, DEPTH), BF16),
             pltpu.VMEM((2, 4, GROUP, 128), BF16),
             pltpu.VMEM((2, 4, GROUP, 128), BF16),
             pltpu.VMEM((2, 4, GROUP, 128), BF16),
+            pltpu.VMEM((2, GROUP, 128), F32),
             pltpu.VMEM((GROUP, FEAT), BF16),
             pltpu.VMEM((2, WIDTH, FEAT), F32),
             pltpu.VMEM((2, 4, 2, GROUP, FEAT), BF16),
@@ -341,12 +398,15 @@
             pltpu.VMEM((2, NX, 16, FEAT), BF16),
             pltpu.VMEM((2, NZ, 16, PIECE), BF16),
             pltpu.VMEM((2, NZ, 16, PIECE), BF16),
-            pltpu.VMEM((2, NZ, 16, PIECE), BF16),
-            pltpu.VMEM((2, NZ, 16, PIECE), BF16),
+            pltpu.VMEM((2, NZ, 16, 256), BF16),
+            pltpu.VMEM((2, NZ, 16, 256), BF16),
+            pltpu.VMEM((2, 16, 128), F32),
             pltpu.VMEM((2, NX, 16, FEAT), BF16),
             pltpu.VMEM((2, NX, 16, FEAT), BF16),
+            pltpu.VMEM((2, FEAT, WIDTH), BF16),
             pltpu.VMEM((2, 2 * NY, 128, 128), BF16),
-            dma((5,)),
+            pltpu.SemaphoreType.REGULAR((2,)),
+            dma((9,)),
             dma((13,)),
             dma((13,)),
             dma((2, NX)),
@@ -363,7 +423,8 @@
         compiler_params=pltpu.CompilerParams(
             collective_id=0, has_side_effects=True, vmem_limit_bytes=58 * 2**20),
         cost_estimate=pl.CostEstimate(flops=10 * 10**9, bytes_accessed=8 * 2**20, transcendentals=0),
-    )(tokens, projection, context_state, norm_gain.reshape(1, -1))
+    )(tokens, projection, jnp.swapaxes(context_state, 1, 2).reshape(128, PAIRS), norm_gain.reshape(1, -1))
+    return jnp.swapaxes(pieces, 0, 1).reshape(128, 2048)
 
 
 def solution(mesh):

time: 75.2 us -> 68 us (0.904)
  Pallas kernels: 70.4 us -> 65.5 us
  local copies, waits for them, and re-layouts: 4.67 us -> 2.32 us
    pallas_call x1, Pallas kernels: 70.4 us -> 65.5 us  [local(): pl.pallas_call(kernel, out_shape=jax.ShapeDtypeStruct((4 * NY, 128, 128),...]
    unnamed x2 -> x0, local copies, waits for them, and re-layouts: 4.67 us -> none
    transpose x0 -> x1, local copies, waits for them, and re-layouts: none -> 1.31 us  [local(): return jnp.swapaxes(pieces, 0, 1).reshape(128, 2048)]
    reshape x0 -> x1, local copies, waits for them, and re-layouts: none -> 1.01 us  [local(): return jnp.swapaxes(pieces, 0, 1).reshape(128, 2048)]
where the time goes in v2:
time: 68 us; the launch traced here: 67.8 us
  Pallas kernels  65.5 us (96%)
  local copies, waits for them, and re-layouts  2.32 us (3%)
    pallas_call x1, Pallas kernels, local(): pl.pallas_call(kernel, out_shape=jax.ShapeDtypeStruct((4 * NY, 128, 128),...  65.5 us

profile of v2, /device:TPU:1, one launch (start us, length us, event | category | flops | bytes accessed | tf_op | source)
XLA Modules:
  0.0 67.8 jit_solution(15620506652462261640)
XLA Ops:
  0.0 65.5 %shard_map.46 = bf16[16,128,128]{2,1,0:T(8,128)(2,1)} custom-call(bf16[128,2048]{1,0:T(8,128)(2,1)} %tok_ref.1, bf16[2048,512]{1,0:T(8,128)(2,1)} %w_hbm.1, f32[128,2080]{1,0:T(8,128)} %bitcast.8, f32[1,256]{1,0:T(1,128)} %bitcast.9), custom_call_target="tpu_custom_call" | custom-call | flops 10000000000 | bytes 8388608 | tf_op jit(solution)/shard_map/pallas_call | solution.py:377
  65.5 1.3 %copy.5 = bf16[128,16,128]{0,2,1:T(8,128)(2,1)S(1)} copy(bf16[128,16,128]{2,0,1:T(8,128)(2,1)} %bitcast.7) | data formatting | bytes 1048576 | tf_op jit(solution)/shard_map/transpose | solution.py:427
  66.8 1.0 %copy.6 = bf16[128,2048]{1,0:T(8,128)(2,1)} copy(bf16[128,2048]{0,1:T(8,128)(2,1)S(1)} %bitcast.6) | data formatting | bytes 1048576 | tf_op jit(solution)/shard_map/reshape | solution.py:427

commit v3 on v2

--- a/solution.py
+++ b/solution.py
@@ -16,8 +16,9 @@
 DEPTH = 2048
 CHUNKS = 17
 FEAT = 128 * CHUNKS
+PARTS = ((0, 1024), (1024, FEAT))
 PAIRS = 2080
-PIECE = 384
+FAR_FIRST_X, FAR_FIRST_Z = (2, 1, 3), (4, 3, 5, 2, 6, 1, 7)
 F32, BF16 = jnp.float32, jnp.bfloat16
 
 
@@ -29,11 +30,10 @@
     return pltpu.roll(value, 128 - amount, 1)
 
 
-def write_features(twice, store):
+def write_features(twice, store, chunks=range(17)):
     base = jnp.where(lanes(twice.shape[0]) < WIDTH, twice, left(twice, 16))
-    for m in range(16):
-        store(m, (base * left(twice, 17 + m)).astype(BF16))
-    store(16, (twice * twice).astype(BF16))
+    for m in chunks:
+        store(m, (base * left(twice, 17 + m) if m < 16 else twice * twice).astype(BF16))
 
 
 def doubled(pair, half):
@@ -122,35 +122,79 @@
     def have(row, half, slot):
         arrived(xall.at[row, half], gs.at[slot], gr.at[slot])
 
-    def project(group, first=False, then=None):
+    def span(half):
+        return pl.ds(half * 128, 128) if isinstance(half, int) else pl.ds(pl.multiple_of(half * 128, 128), 128)
+
+    def project(group, first=False, then=None, rest=None):
         def rows():
             return xall[pl.ds(2 * group, 2)].reshape(GROUP, DEPTH)
 
-        @stage
-        def _():
-            made = jnp.dot(rows(), w_v[0], preferred_element_type=F32).astype(BF16).astype(F32)
+        def key_values(half):
+            block = xall[2 * group + half]
+            made = jnp.dot(block, w_v[0], preferred_element_type=F32).astype(BF16).astype(F32)
             for h in range(2):
-                kv_v[h] = made[:, 128 * h:128 * h + 128]
-
-        for h in range(2):
-            @stage
-            def _():
-                pair = kv_v[h]
-                twice = doubled(pair, 0)
-
-                def store(m, value):
-                    phik[:, 128 * m:128 * m + 128] = value
-
-                write_features(twice, store)
-                values = pair.T[WIDTH:].astype(BF16)
-                update = jnp.dot(values, phik[...], preferred_element_type=F32)
-                if first:
-                    state[h] = update
-                else:
-                    state[h] += update
-
-            if then is not None:
-                then(h)
+                kv_v[h, span(half)] = made[:, 128 * h:128 * h + 128]
+
+        def expand(h, half):
+            def store(m, value):
+                phik[h, span(half), 128 * m:128 * m + 128] = value
+
+            write_features(doubled(kv_v[h, span(half)], 0), store)
+
+        def add(h, part):
+            lo, hi = PARTS[part]
+            values = kv_v[h].T[WIDTH:].astype(BF16)
+            update = jnp.dot(values, phik[h, :, lo:hi], preferred_element_type=F32)
+            if first:
+                state[h, :, lo:hi] = update
+            else:
+                state[h, :, lo:hi] += update
+
+        if then is None:
+            @stage
+            def _():
+                made = jnp.dot(rows(), w_v[0], preferred_element_type=F32).astype(BF16).astype(F32)
+                for h in range(2):
+                    kv_v[h] = made[:, 128 * h:128 * h + 128]
+                    for half in range(2):
+                        expand(h, half)
+                    add(h, 0)
+                    add(h, 1)
+        else:
+            @stage
+            def _():
+                key_values(core)
+                expand(0, core)
+                expand(1, core)
+
+            rest()
+
+            @stage
+            def _():
+                key_values(1 - core)
+                expand(0, 1 - core)
+                add(0, 0)
+
+            then(0, 0)
+
+            @stage
+            def _():
+                add(0, 1)
+                expand(1, 1 - core)
+
+            then(0, 1)
+
+            @stage
+            def _():
+                add(1, 0)
+
+            then(1, 0)
+
+            @stage
+            def _():
+                add(1, 1)
+
+            then(1, 1)
 
         @stage
         def _():
@@ -222,64 +266,79 @@
     have(s_up, high, 8)
     have(s_up, low, 10)
     project(up)
+    @pl.when(core == 1)
+    def _():
+        pl.semaphore_wait(barrier, 2 * (NX - 1 + NZ - 1))
+        pl.semaphore_signal(met.at[1], inc=1, device_id=sib, device_id_type=MESH)
+
+    @pl.when(core == 0)
+    def _():
+        pl.semaphore_wait(met.at[1], 1)
+
     have(h_far, low, 5)
     pass_on(h_far, low, 11, sib)
     have(h_far, high, 6)
     pass_on(h_far, high, 12, sib)
-    have(s_far, low, 11)
-    have(s_far, high, 12)
-
-    def x_out(h):
-        xs[h] = state[h].reshape(NX, 16, FEAT).astype(BF16)
-        xr[h, x] = xs[h, x]
+
+    def x_out(h, part):
+        lo, hi = PARTS[part]
+        c = 2 * h + part
+        xs[part][h] = state[h, :, lo:hi].reshape(NX, 16, hi - lo).astype(BF16)
+        xr[part][h, x] = xs[part][h, x]
+        for k in FAR_FIRST_X:
+            there = (x + k) % NX
+            send(xs[part].at[h, there], xr[part].at[h, x], xs_sem.at[c, k], xr_sem.at[c, k], (z * NX + there, me_head))
+
+    def x_in(h, part):
+        c = 2 * h + part
         for k in range(1, NX):
-            there = (x + k) % NX
-            send(xs.at[h, there], xr.at[h, x], xs_sem.at[h, k], xr_sem.at[h, k], (z * NX + there, me_head))
-
-    def x_in(h):
+            arrived(xr[part].at[h, (x + NX - k) % NX], xs_sem.at[c, k], xr_sem.at[c, k])
+        total = xr[part][h, 0].astype(F32)
         for k in range(1, NX):
-            arrived(xr.at[h, (x + NX - k) % NX], xs_sem.at[h, k], xr_sem.at[h, k])
-        total = xr[h, 0].astype(F32)
-        for k in range(1, NX):
-            total += xr[h, k].astype(F32)
+            total += xr[part][h, k].astype(F32)
         total = total.astype(BF16)
         for k in range(NZ):
-            zs[h, k] = jnp.concatenate([total[:, 256 * k:256 * k + 256], total[:, 2048:]], axis=1)
-        zr[h, z] = zs[h, z]
+            piece = total[:, 128 * k:128 * k + 128]
+            zs[part][h, k] = piece if part == 0 else jnp.concatenate([piece, total[:, 1024:]], axis=1)
+        zr[part][h, z] = zs[part][h, z]
+        for k in FAR_FIRST_Z:
+            there = (z + k) % NZ
+            send(zs[part].at[h, there], zr[part].at[h, z], zs_sem.at[c, k], zr_sem.at[c, k], (there * NX + x, me_head))
+
+    def z_in(h, part):
+        c = 2 * h + part
         for k in range(1, NZ):
-            there = (z + k) % NZ
-            send(zs.at[h, there], zr.at[h, z], zs_sem.at[h, k], zr_sem.at[h, k], (there * NX + x, me_head))
-
-    def z_in(h):
-        for k in range(1, NZ):
-            arrived(zr.at[h, (z + NZ - k) % NZ], zs_sem.at[h, k], zr_sem.at[h, k])
-        running = jnp.zeros((16, 256), F32)
+            arrived(zr[part].at[h, (z + NZ - k) % NZ], zs_sem.at[c, k], zr_sem.at[c, k])
+        running = jnp.zeros((16, 128), F32)
         tail = jnp.zeros((16, 128), F32)
         for k in range(NZ):
-            es[h, k] = running.astype(BF16)
-            running += zr[h, k, :, :256].astype(F32)
-            tail += jnp.where(k < z, zr[h, k, :, 256:].astype(F32), 0.0)
-        tails[h] = tail
-        er[h, z] = es[h, z]
+            es[part][h, k] = running.astype(BF16)
+            running += zr[part][h, k, :, :128].astype(F32)
+            if part == 1:
+                tail += jnp.where(k < z, zr[part][h, k, :, 128:].astype(F32), 0.0)
+        if part == 1:
+            tails[h] = tail
+        er[part][h, z] = es[part][h, z]
+        for k in FAR_FIRST_Z:
+            there = (z + k) % NZ
+            send(es[part].at[h, there], er[part].at[h, z], es_sem.at[c, k], er_sem.at[c, k], (there * NX + x, me_head))
+
+    def e_in(h, part):
+        lo, hi = PARTS[part]
+        c = 2 * h + part
         for k in range(1, NZ):
-            there = (z + k) % NZ
-            send(es.at[h, there], er.at[h, z], es_sem.at[h, k], er_sem.at[h, k], (there * NX + x, me_head))
-
-    def e_in(h):
-        for k in range(1, NZ):
-            arrived(er.at[h, (z + NZ - k) % NZ], es_sem.at[h, k], er_sem.at[h, k])
-        earlier = jnp.concatenate(
-            [er[h, k].astype(F32) for k in range(NZ)] + [tails[h]], axis=1)
-        before = ctx_t[4 * h + x] * single_weight
-        running = earlier
+            arrived(er[part].at[h, (z + NZ - k) % NZ], es_sem.at[c, k], er_sem.at[c, k])
+        running = jnp.concatenate(
+            [er[part][h, k].astype(F32) for k in range(NZ)] + ([tails[h]] if part == 1 else []), axis=1)
+        before = ctx_t[4 * h + x, :, lo:hi] * single_weight[:, lo:hi]
         for k in range(NX):
-            ps[h, k] = (before + running * square_weight).astype(BF16)
+            ps[part][h, k] = (before + running * square_weight[:, lo:hi]).astype(BF16)
             if k < NX - 1:
-                running += xr[h, k].astype(F32)
-        pt[h, x] = ps[h, x]
-        for k in range(1, NX):
+                running += xr[part][h, k].astype(F32)
+        pt[part][h, x] = ps[part][h, x]
+        for k in FAR_FIRST_X:
             there = (x + k) % NX
-            send(ps.at[h, there], pt.at[h, x], ps_sem.at[h, k], pr_sem.at[h, k], (z * NX + there, me_head))
+            send(ps[part].at[h, there], pt[part].at[h, x], ps_sem.at[c, k], pr_sem.at[c, k], (z * NX + there, me_head))
 
     causal = (lax.broadcasted_iota(jnp.int32, (GROUP, GROUP), 1)
               <= lax.broadcasted_iota(jnp.int32, (GROUP, GROUP), 0))
@@ -307,23 +366,30 @@
 
     kept = []
 
-    def finish(h):
+    def finish(h, part):
+        lo, hi = PARTS[part]
+        c = 2 * h + part
         for k in range(1, NX):
-            arrived(pt.at[h, (x + NX - k) % NX], ps_sem.at[h, k], pr_sem.at[h, k])
-        turned[h] = pt[h].reshape(WIDTH, FEAT).astype(F32).T.astype(BF16)
+            arrived(pt[part].at[h, (x + NX - k) % NX], ps_sem.at[c, k], pr_sem.at[c, k])
+        turned[h, lo:hi] = pt[part][h].reshape(WIDTH, hi - lo).astype(F32).T.astype(BF16)
         for k in (2, 1, 3, 0):
             i = (y + k) % NY
 
             @stage
             def _():
                 carried = jnp.dot(
-                    phiq[h, i].reshape(2 * GROUP, FEAT), turned[h], preferred_element_type=F32)
+                    phiq[h, i, :, :, lo:hi].reshape(2 * GROUP, hi - lo), turned[h, lo:hi], preferred_element_type=F32)
                 combined = carried + comb[h, i].reshape(2 * GROUP, 128)[:, :WIDTH]
+                if part == 0:
+                    comb[h, i, :, :, :WIDTH] = combined.reshape(2, GROUP, WIDTH)
+                    return
                 inverse = lax.rsqrt(jnp.mean(combined * combined, -1, keepdims=True) + 1e-05)
                 made = combined * inverse
                 both = jnp.concatenate([made[:GROUP], made[GROUP:]], axis=1) * gain_ref[:, 128 * h:128 * h + 128]
                 ob[h, pl.ds(2 * i, 2)] = both.astype(BF16).reshape(2, 128, 128)
 
+            if part == 0:
+                continue
             for d in range(2):
                 there = i * 2 + (core + d) % 2
                 if k == 0 and d == 0:
@@ -334,32 +400,22 @@
                     send(ob.at[h, there], out_ref.at[2 * me_head + h],
                          os_sem.at[h, 2 * k + d], or_sem.at[h, 2 * k + d], (me_ctx, there))
 
-    @pl.when(core == 1)
-    def _():
-        pl.semaphore_wait(barrier, 2 * (NX - 1 + NZ - 1))
-        pl.semaphore_signal(met.at[1], inc=1, device_id=sib, device_id_type=MESH)
-
-    @pl.when(core == 0)
-    def _():
-        pl.semaphore_wait(met.at[1], 1)
-
-    project(far, then=x_out)
-    stage(functools.partial(tile, 0, 0))
-    stage(functools.partial(tile, 0, 1))
-    stage(functools.partial(tile, 0, 2))
-    x_in(0)
-    stage(functools.partial(tile, 0, 3))
-    x_in(1)
-    stage(functools.partial(tile, 1, 0))
-    stage(functools.partial(tile, 1, 1))
-    z_in(0)
-    stage(functools.partial(tile, 1, 2))
-    z_in(1)
-    stage(functools.partial(tile, 1, 3))
-    e_in(0)
-    e_in(1)
-    finish(0)
-    finish(1)
+    def rest():
+        have(s_far, low, 11)
+        have(s_far, high, 12)
+
+    project(far, then=x_out, rest=rest)
+    order = [(h, part) for h in range(2) for part in range(2)]
+    tiles = [(h, i) for h in range(2) for i in range(4)]
+    for step, counts in ((x_in, (2, 1, 1, 1)), (z_in, (1, 1, 1, 0))):
+        for now, count in zip(order, counts):
+            for _ in range(count):
+                stage(functools.partial(tile, *tiles.pop(0)))
+            step(*now)
+    for now in order:
+        e_in(*now)
+    for now in order:
+        finish(*now)
     for copy in kept:
         copy.wait()
     for h in range(2):
@@ -374,6 +430,10 @@
 
 def local(tokens, projection, context_state, norm_gain):
     dma = pltpu.SemaphoreType.DMA
+
+    def parted(count, *widths):
+        return [pltpu.VMEM((2, count, 16, width), BF16) for width in widths]
+
     pieces = pl.pallas_call(
         kernel,
         out_shape=jax.ShapeDtypeStruct((4 * NY, 128, 128), BF16),
@@ -387,36 +447,36 @@
             pltpu.VMEM((2, 4, GROUP, 128), BF16),
             pltpu.VMEM((2, 4, GROUP, 128), BF16),
             pltpu.VMEM((2, GROUP, 128), F32),
-            pltpu.VMEM((GROUP, FEAT), BF16),
+            pltpu.VMEM((2, GROUP, FEAT), BF16),
             pltpu.VMEM((2, WIDTH, FEAT), F32),
             pltpu.VMEM((2, 4, 2, GROUP, FEAT), BF16),
             pltpu.VMEM((2, 4, 2, GROUP, 128), F32),
             pltpu.VMEM((64 * 129 + 8, 128), F32),
             pltpu.VMEM((FEAT, 128), F32),
             pltpu.VMEM((8, 16, FEAT), F32),
-            pltpu.VMEM((2, NX, 16, FEAT), BF16),
-            pltpu.VMEM((2, NX, 16, FEAT), BF16),
-            pltpu.VMEM((2, NZ, 16, PIECE), BF16),
-            pltpu.VMEM((2, NZ, 16, PIECE), BF16),
-            pltpu.VMEM((2, NZ, 16, 256), BF16),
-            pltpu.VMEM((2, NZ, 16, 256), BF16),
+            parted(NX, 1024, 1152),
+            parted(NX, 1024, 1152),
+            parted(NZ, 128, 256),
+            parted(NZ, 128, 256),
+            parted(NZ, 128, 128),
+            parted(NZ, 128, 128),
             pltpu.VMEM((2, 16, 128), F32),
-            pltpu.VMEM((2, NX, 16, FEAT), BF16),
-            pltpu.VMEM((2, NX, 16, FEAT), BF16),
+            parted(NX, 1024, 1152),
+            parted(NX, 1024, 1152),
             pltpu.VMEM((2, FEAT, WIDTH), BF16),
             pltpu.VMEM((2, 2 * NY, 128, 128), BF16),
             pltpu.SemaphoreType.REGULAR((2,)),
             dma((9,)),
             dma((13,)),
             dma((13,)),
-            dma((2, NX)),
-            dma((2, NX)),
-            dma((2, NZ)),
-            dma((2, NZ)),
-            dma((2, NZ)),
-            dma((2, NZ)),
-            dma((2, NX)),
-            dma((2, NX)),
+            dma((4, NX)),
+            dma((4, NX)),
+            dma((4, NZ)),
+            dma((4, NZ)),
+            dma((4, NZ)),
+            dma((4, NZ)),
+            dma((4, NX)),
+            dma((4, NX)),
             dma((2, 2 * NY)),
             dma((2, 2 * NY)),
         ],

time: 68 us -> 66.4 us (0.976)
  Pallas kernels: 65.5 us -> 63.9 us
    pallas_call x1, Pallas kernels: 65.5 us -> 63.9 us  [local(): pl.pallas_call(kernel, out_shape=jax.ShapeDtypeStruct((4 * NY, 128, 128),...]
where the time goes in v3:
time: 66.4 us; the launch traced here: 66.2 us
  Pallas kernels  63.9 us (96%)
  local copies, waits for them, and re-layouts  2.32 us (3%)
    pallas_call x1, Pallas kernels, local(): pl.pallas_call(kernel, out_shape=jax.ShapeDtypeStruct((4 * NY, 128, 128),...  63.9 us

profile of v3, /device:TPU:1, one launch (start us, length us, event | category | flops | bytes accessed | tf_op | source)
XLA Modules:
  0.0 66.2 jit_solution(8066746863413059205)
XLA Ops:
  0.0 63.9 %shard_map.46 = bf16[16,128,128]{2,1,0:T(8,128)(2,1)} custom-call(bf16[128,2048]{1,0:T(8,128)(2,1)} %tok_ref.1, bf16[2048,512]{1,0:T(8,128)(2,1)} %w_hbm.1, f32[128,2080]{1,0:T(8,128)} %bitcast.8, f32[1,256]{1,0:T(1,128)} %bitcast.9), custom_call_target="tpu_custom_call" | custom-call | flops 10000000000 | bytes 8388608 | tf_op jit(solution)/shard_map/pallas_call | solution.py:437
  63.9 1.3 %copy.5 = bf16[128,16,128]{0,2,1:T(8,128)(2,1)S(1)} copy(bf16[128,16,128]{2,0,1:T(8,128)(2,1)} %bitcast.7) | data formatting | bytes 1048576 | tf_op jit(solution)/shard_map/transpose | solution.py:487
  65.2 1.0 %copy.6 = bf16[128,2048]{1,0:T(8,128)(2,1)} copy(bf16[128,2048]{0,1:T(8,128)(2,1)S(1)} %bitcast.6) | data formatting | bytes 1048576 | tf_op jit(solution)/shard_map/reshape | solution.py:487
